TPU v7x, 32 devices: a whole 2x2x4 slice. The times are simulated.
32 devices in a mesh: tm: 8 (over z, x), sta: 4 (over y, core).
Axes of the slice: x: 2, y: 2, z: 4, core: 2. Of those that a mesh axis runs over, the one named last changes fastest.
Arguments:
- voltages: bfloat16 [2, 4, 64, 262144], P(None, None, 'sta', 'tm'), may hold values from -6 to 6
- sample_delay: int32 [64, 8], P('sta', 'tm'), may hold values from 0 to 8192, as said below
- frac_index: int32 [64, 8], P('sta', 'tm'), may hold values from 0 to 63
- phase_index: int32 [4, 64, 8], P(None, 'sta', 'tm'), may hold values from 0 to 1023
- fringe_rate: float32 [4, 64], P(None, 'sta'), may hold values from -3 to 3
Outputs:
- visibilities: float32 [4, 16384, 64, 128], P(None, ('tm', 'sta'))
Inputs may be any that keep to these rules, and one draw needn't show every extreme that they name: `sample_delay`: the largest delay, 8192, occurs in every draw.
All inputs are finite; a program needn't handle non-finite values.
Results may differ from a plain program's by a relative error of at most 0.0089.
Values may be sent and summed in bfloat16 or wider, within the bound.
A program may use at most 256 MiB of HBM per device.

v0:
```python
import math
import jax
import jax.numpy as jnp
from jax import lax
from jax.sharding import PartitionSpec as P

CHANNELS = 16384
RADIX_A = 128
RADIX_B = 128
TAPS = 32
NFRAC = 64
NPHASE = 1024
MAXD = 8192


def shifted(value, axis, steps):
    count = lax.axis_size(axis)
    first, last = (max(0, -steps), min(count, count - steps))
    return lax.ppermute(value, axis, [(source, source + steps) for source in range(first, last)])


def toeplitz_of(fraction_index):
    inputs_at = jnp.arange(256, dtype=jnp.int32)
    outputs_at = jnp.arange(128, dtype=jnp.int32)
    distance = inputs_at[:, None] - outputs_at[None, :]
    inside = (distance >= 0) & (distance < TAPS)
    fraction = fraction_index.astype(jnp.float32) / NFRAC
    offset = distance.astype(jnp.float32)
    centre = offset[None, :, :] - (TAPS // 2 - 1) - fraction[:, None, None]
    window_taper = 0.5 - 0.5 * jnp.cos(2.0 * jnp.pi * (offset + 0.5) / TAPS)
    values = jnp.sinc(centre) * window_taper[None, :, :]
    return jnp.where(inside[None, :, :], values, 0.0).astype(jnp.bfloat16)


def filter_rows(source, starts, kernel, sample_count):
    slicer = jax.vmap(
        lambda series, start_at: lax.dynamic_slice_in_dim(
            series, start_at, sample_count + 128, axis=1
        ),
        in_axes=(1, 0),
        out_axes=1,
    )
    pieces = slicer(source, starts)
    row_count = pieces.shape[1]
    blocks = sample_count // 128
    tiles = pieces.reshape(2, row_count, blocks + 1, 128)
    upper = jnp.einsum(
        "crnp,rpv->crnv", tiles[:, :, :blocks], kernel[:, :128], preferred_element_type=jnp.float32
    )
    lower = jnp.einsum(
        "crnp,rpv->crnv", tiles[:, :, 1:], kernel[:, 128:], preferred_element_type=jnp.float32
    )
    return (upper + lower).reshape(2, row_count, sample_count)


def rotate_rows(filtered, phase_rows, rate_rows, slice_length):
    sample_count = filtered.shape[-1]
    position = jnp.arange(sample_count, dtype=jnp.int32).astype(jnp.float32) / slice_length
    cycles = (
        phase_rows.astype(jnp.float32)[:, None] / NPHASE + rate_rows[:, None] * position[None, :]
    )
    phase_angle = 2.0 * jnp.pi * cycles
    cosine = jnp.cos(phase_angle)
    sine_value = jnp.sin(phase_angle)
    real_part = filtered[0] * cosine + filtered[1] * sine_value
    imag_part = filtered[1] * cosine - filtered[0] * sine_value
    return jnp.stack([real_part, imag_part]).astype(jnp.bfloat16)


def rotation_table(indices, radix_size):
    product = indices[:, None] * indices[None, :] % radix_size
    table_angle = product.astype(jnp.float32) * (2.0 * math.pi / radix_size)
    scaling = 1.0 / math.sqrt(radix_size)
    cosine = jnp.cos(table_angle) * scaling
    sine_value = jnp.sin(table_angle) * scaling
    stacked = jnp.stack(
        [jnp.stack([cosine, sine_value], axis=1), jnp.stack([-sine_value, cosine], axis=1)], axis=0
    )
    return stacked.astype(jnp.bfloat16)


def dft_tables():
    along_a = jnp.arange(RADIX_A, dtype=jnp.int32)
    along_b = jnp.arange(RADIX_B, dtype=jnp.int32)
    first_table = rotation_table(along_a, RADIX_A)
    second_table = rotation_table(along_b, RADIX_B)
    product = along_a[:, None] * along_b[None, :] % CHANNELS
    twist_angle = product.astype(jnp.float32) * (2.0 * math.pi / CHANNELS)
    twiddle = jnp.stack([jnp.cos(twist_angle), jnp.sin(twist_angle)])
    return (first_table, twiddle, second_table)


def transform(rotated, tables, block_width):
    first_table, twiddle, second_table = tables
    row_count = rotated.shape[1]
    frames = rotated.shape[2] // CHANNELS
    arranged = rotated.reshape(2, row_count, frames, RADIX_A, RADIX_B)
    section_half = jnp.einsum(
        "pkcn,crfnm->prfkm", first_table, arranged, preferred_element_type=jnp.float32
    )
    real_part = section_half[0] * twiddle[0] + section_half[1] * twiddle[1]
    imag_part = section_half[1] * twiddle[0] - section_half[0] * twiddle[1]
    partial_value = jnp.stack([real_part, imag_part]).astype(jnp.bfloat16)
    block_count = CHANNELS // block_width
    if block_width <= RADIX_A:
        split_rows = partial_value.reshape(
            2, row_count, frames, RADIX_A // block_width, block_width, RADIX_B
        )
        spectrum = jnp.einsum(
            "qjpm,prfakm->rfjaqk", second_table, split_rows, preferred_element_type=jnp.float32
        )
    else:
        split_table = second_table.reshape(2, block_count, block_width // RADIX_A, 2, RADIX_B)
        spectrum = jnp.einsum(
            "qJjpm,prfkm->rfJqjk", split_table, partial_value, preferred_element_type=jnp.float32
        )
    return spectrum.astype(jnp.bfloat16).reshape(row_count, frames, block_count, 2 * block_width)


def correlate(spectra):
    frame_total = spectra.shape[2]
    turned = jnp.stack([-spectra[:, :, :, 1], spectra[:, :, :, 0]], axis=3)
    partner = jnp.concatenate([spectra, turned], axis=1)
    summed = jnp.einsum("bifck,bjfck->bkij", spectra, partner, preferred_element_type=jnp.float32)
    return summed / frame_total


def local(voltages, sample_delay, frac_index, phase_index, fringe_rate):
    band_count = voltages.shape[1]
    station_count = voltages.shape[2]
    length = voltages.shape[3]
    frames = length // CHANNELS
    row_count = band_count * station_count
    flattened = voltages.reshape(2, row_count, length)
    delays = jnp.broadcast_to(sample_delay[:, 0][None, :], (band_count, station_count)).reshape(
        row_count
    )
    kernel = toeplitz_of(frac_index[:, 0])
    kernel_rows = jnp.broadcast_to(kernel[None], (band_count,) + kernel.shape).reshape(
        (row_count,) + kernel.shape[1:]
    )
    phase_rows = phase_index[:, :, 0].reshape(row_count)
    rate_rows = fringe_rate.reshape(row_count)
    rim_width = MAXD + TAPS - 1
    following = shifted(flattened[:, :, :rim_width], "tm", -1)
    padding = jnp.zeros((2, row_count, 129 - TAPS), flattened.dtype)
    source = jnp.concatenate([flattened, following, padding], axis=2)
    rotated = rotate_rows(
        filter_rows(source, delays, kernel_rows, length), phase_rows, rate_rows, length
    )
    slices = lax.axis_size("tm")
    groups = lax.axis_size("sta")
    block_width = CHANNELS // (slices * groups)
    spectra = transform(rotated, dft_tables(), block_width)
    packed = spectra.reshape(band_count, station_count, frames, slices, groups, 2 * block_width)
    received = lax.all_to_all(
        lax.all_to_all(packed, "tm", split_axis=3, concat_axis=2, tiled=True),
        "sta",
        split_axis=4,
        concat_axis=1,
        tiled=True,
    )
    gathered = received.reshape(band_count, station_count * groups, slices * frames, 2, block_width)
    return correlate(gathered)


def solution(mesh):
    return jax.shard_map(
        local,
        mesh=mesh,
        in_specs=(
            P(None, None, "sta", "tm"),
            P("sta", "tm"),
            P("sta", "tm"),
            P(None, "sta", "tm"),
            P(None, "sta"),
        ),
        out_specs=P(None, ("tm", "sta"), None, None),
        check_vma=False,
    )
```

profile of v0, /device:TPU:0, one launch (start us, length us, event | category | flops | bytes accessed | tf_op | source)
XLA Modules:
  0.0 952.2 jit_solution(5046426309771215276)
XLA Ops:
  0.0 14.6 %copy.28 = bf16[2,4,16,32768]{3,0,2,1:T(2,128)(2,1)S(1)} copy(bf16[2,4,16,32768]{3,2,1,0:T(8,128)(2,1)} %param.5) | data formatting | bytes 16777216 | tf_op args[0]
  19.4 7.0 constant_dynamic-update-slice_fusion
  32.5 36.5 %collective-permute-done = bf16[2,64,8223]{2,0,1:T(2,128)(2,1)S(1)} collective-permute-done((bf16[2,64,8223]{2,0,1:T(2,128)(2,1)}, bf16[2,64,8223]{2,0,1:T(2,128)(2,1)S(1)}, u32[]{:S(2)}, u32[]{:S(2)}) %collective-permute-start) | collective-permute-done | bytes 2105120 | tf_op jit(solution)/shard_map/ppermute | solution.py:19
  68.9 60.9 %dynamic-update-slice.3 = bf16[2,64,41088]{2,0,1:T(2,128)(2,1)} dynamic-update-slice(bf16[2,64,41088]{2,0,1:T(2,128)(2,1)} %constant_dynamic-update-slice_fusion, bf16[2,64,8223]{2,0,1:T(2,128)(2,1)S(1)} %collective-permute-done, s32[]{} %constant.144, s32[]{} %constant.144, s32[]{} %constant.145) | dynamic-update-slice | bytes 4210180
  129.9 10.2 %dynamic-update-slice.4 = bf16[2,64,41088]{2,0,1:T(2,128)(2,1)} dynamic-update-slice(bf16[2,64,41088]{2,0,1:T(2,128)(2,1)} %dynamic-update-slice.3, bf16[2,64,97]{2,0,1:T(2,128)(2,1)S(1)} %broadcast_in_dim.25, s32[]{} %constant.144, s32[]{} %constant.144, s32[]{} %constant.146) | dynamic-update-slice | bytes 49668 | tf_op jit(solution)/shard_map/concatenate | solution.py:147
  140.0 234.9 %while.1 = (s32[]{:T(128)}, bf16[64,2,41088]{2,1,0:T(2,128)(2,1)}, s32[64,3]{0,1:T(4,128)S(1)}, bf16[64,2,32896]{2,1,0:T(2,128)(2,1)}, s32[]{:T(128)}) while((s32[]{:T(128)}, bf16[64,2,41088]{2,1,0:T(2,128)(2,1)}, s32[64,3]{0,1:T(4,128)S(1)}, bf16[64,2,32896]{2,1,0:T(2,128)(2,1)}, s32[]{:T(128)}) %tuple.32), condition=%wide.while_cond, body=%wide.while_body.sunk | while | flops 2 | bytes 264309 | solution.py:37
  162.7 3.0 dynamic-slice_dynamic-update-slice_fusion.2
  188.4 3.0 dynamic-slice_dynamic-update-slice_fusion.2
  199.4 3.0 dynamic-slice_dynamic-update-slice_fusion.2
  265.5 3.0 dynamic-slice_dynamic-update-slice_fusion.2
  374.9 14.2 %reshape.521 = bf16[2,64,257,128]{3,2,0,1:T(8,128)(2,1)} reshape(bf16[2,64,32896]{2,0,1:T(2,128)(2,1)} %bitcast.99) | data formatting | bytes 16842752 | tf_op jit(solution)/shard_map/reshape | solution.py:46
  391.6 11.9 %fusion.6 = f32[64,128,2,256]{3,1,2,0:T(8,128)} fusion(bf16[2,64,257,128]{3,2,0,1:T(8,128)(2,1)} %reshape.521, bf16[64,256,128]{1,2,0:T(8,128)(2,1)S(1)} %bitcast.97), kind=kOutput, calls=%fused_computation.13 | convolution fusion | flops 1073741824 | bytes 27262976 | tf_op jit(solution)/shard_map/crnp,rpv->crnv/dot_general | solution.py:47
  403.5 16.7 %add_bitcast_fusion = f32[2,64,256,128]{2,3,0,1:T(8,128)} fusion(f32[64,128,2,256]{3,1,2,0:T(8,128)} %fusion.6, bf16[2,64,257,128]{3,2,0,1:T(8,128)(2,1)} %reshape.521, bf16[64,256,128]{1,2,0:T(8,128)(2,1)} %bitcast.98), kind=kOutput, calls=%fused_computation.9 | convolution fusion | flops 1077936128 | bytes 44040192 | tf_op jit(solution)/shard_map/crnp,rpv->crnv/dot_general | solution.py:50
  420.2 11.1 %fusion.78 = (f32[1,64,256,128]{2,3,0,1:T(8,128)}, f32[1,64,256,128]{2,3,0,1:T(8,128)}) fusion(f32[2,64,256,128]{2,3,0,1:T(8,128)} %add_bitcast_fusion), kind=kLoop, calls=%fused_computation.130 | loop fusion | bytes 33554432 | tf_op jit(solution)/shard_map/slice | solution.py:65
  431.2 10.8 %squeeze.4 = f32[1,64,2,128,128]{3,2,4,1,0:T(2,128)} reshape(f32[1,64,256,128]{2,3,0,1:T(8,128)} %get-tuple-element.29) | data formatting | bytes 16777216 | tf_op jit(solution)/shard_map/squeeze | solution.py:65
  442.1 10.8 %squeeze.5 = f32[1,64,2,128,128]{3,2,4,1,0:T(2,128)} reshape(f32[1,64,256,128]{2,3,0,1:T(8,128)} %get-tuple-element.30) | data formatting | bytes 16777216 | tf_op jit(solution)/shard_map/squeeze | solution.py:65
  452.8 35.4 %add_convert_fusion.1 = (bf16[1,64,2,128,128]{3,4,0,2,1:T(8,128)(2,1)S(1)}, bf16[1,64,2,128,128]{3,4,0,2,1:T(8,128)(2,1)}) fusion(f32[1,64,2,128,128]{3,2,4,1,0:T(2,128)} %squeeze.5, f32[1,64,2,128,128]{3,2,4,1,0:T(2,128)} %squeeze.4, f32[2,128,128]{1,2,0:T(8,128)S(1)} %convert_multiply_fusion, f32[64]{0:T(128)S(1)} %mul.534, f32[64]{0:T(128)S(1)} %div.46), kind=kLoop, calls=%fused_computation.24 | loop fusion | flops 23068672 | bytes 25297408 | tf_op jit(solution)/shard_map/convert.16
  488.2 4.6 convolution_bitcast_fusion
  492.8 3.8 add_convert_fusion
  496.6 4.6 fusion.14
  501.2 9.8 %copy.37 = bf16[64,2,32,2,4,128]{5,4,3,0,2,1:T(4,128)(2,1)} copy(bf16[64,2,32,2,4,128]{5,2,4,3,1,0:T(8,128)(2,1)S(1)} %fusion.14) | data formatting | bytes 16777216 | tf_op jit(solution)/shard_map/convert_element_type | solution.py:117
  511.1 14.3 %reshape_reshape.3 = bf16[4,16,2,8,4,1024]{5,1,0,4,3,2:T(8,128)(2,1)} reshape(bf16[64,2,32,2,4,128]{5,4,3,0,2,1:T(4,128)(2,1)} %copy.37) | data formatting | bytes 16777216 | tf_op jit(solution)/shard_map/reshape;reshape | solution.py:155
  525.4 8.7 copy.38
  534.1 188.9 %all_to_all.33 = bf16[4,16,2,8,4,1024]{5,1,0,4,2,3:T(8,128)(2,1)} all-to-all(bf16[4,16,2,8,4,1024]{5,1,0,4,2,3:T(8,128)(2,1)} %copy.38), channel_id=1, replica_groups=mesh['tm'=8,'sta'=4] {'tm'}, dimensions={3} | all-to-all | bytes 16777216 | tf_op jit(solution)/shard_map/all_to_all | solution.py:157
  723.0 8.7 copy.39
  731.7 8.5 copy.40
  740.2 100.8 %all_to_all.34 = bf16[4,16,16,1,4,1024]{5,1,2,0,3,4:T(8,128)(2,1)} all-to-all(bf16[4,16,16,1,4,1024]{5,1,2,0,3,4:T(8,128)(2,1)} %copy.40), channel_id=1, replica_groups=mesh['tm'=8,'sta'=4] {'sta'}, dimensions={4} | all-to-all | bytes 16777216 | tf_op jit(solution)/shard_map/all_to_all | solution.py:156
  841.0 12.8 %copy.41 = bf16[4,4,16,16,1,1,1024]{6,3,2,1,0,5,4:T(8,128)(2,1)} copy(bf16[4,4,16,16,1,1,1024]{6,2,3,0,1,5,4:T(8,128)(2,1)} %bitcast.96) | data formatting | bytes 16777216 | tf_op jit(solution)/shard_map/all_to_all | solution.py:156
  853.9 14.5 %reshape.488 = bf16[4,64,16,2,512]{4,3,2,1,0:T(2,128)(2,1)} reshape(bf16[4,4,16,16,1,1,1024]{6,3,2,1,0,5,4:T(8,128)(2,1)} %copy.41) | data formatting | bytes 16777216 | tf_op jit(solution)/shard_map/reshape | solution.py:163
  868.3 28.7 %copy.45 = bf16[4,64,16,2,512]{1,2,3,4,0:T(8,128)(2,1)} copy(bf16[4,64,16,2,512]{4,3,2,1,0:T(2,128)(2,1)} %reshape.488) | data formatting | bytes 16777216 | tf_op jit(solution)/shard_map/reshape | solution.py:163
  897.1 11.6 %slice_negate_fusion = (bf16[4,64,16,1,512]{1,2,3,4,0:T(8,128)(2,1)}, bf16[4,64,16,1,512]{1,2,3,4,0:T(8,128)(2,1)}) fusion(bf16[4,64,16,2,512]{1,2,3,4,0:T(8,128)(2,1)} %copy.45), kind=kLoop, calls=%fused_computation.11 | loop fusion | flops 2097152 | bytes 16777216 | tf_op jit(solution)/shard_map/neg | solution.py:122
  908.7 43.3 %bitcast_multiply_fusion = f32[4,512,64,128]{3,2,1,0:T(8,128)} fusion(bf16[4,64,16,2,512]{1,2,3,4,0:T(8,128)(2,1)} %copy.45, bf16[4,64,16,1,512]{1,2,3,4,0:T(8,128)(2,1)} %get-tuple-element.28, bf16[4,64,16,1,512]{1,2,3,4,0:T(8,128)(2,1)} %get-tuple-element.27), kind=kOutput, calls=%fused_computation.2 | convolution fusion | flops 1140850688 | bytes 83886080 | tf_op jit(solution)/shard_map/bifck,bjfck->bkij/dot_general | solution.py:124
  (228 shorter events, 235.9 us)
Async XLA Ops:
  17.6 51.4 %collective-permute-start = (bf16[2,64,8223]{2,0,1:T(2,128)(2,1)}, bf16[2,64,8223]{2,0,1:T(2,128)(2,1)S(1)}, u32[]{:S(2)}, u32[]{:S(2)}) collective-permute-start(bf16[2,64,8223]{2,0,1:T(2,128)(2,1)} %slice.65), channel_id=1, source_target_pairs={{4,0},{8,4},{12,8},{16,12},{20,16},{24,20},{28,24},{5,1},{9,5},{13... | collective-permute-start | bytes 6315272 | tf_op jit(solution)/shard_map/ppermute | solution.py:19
  19.3 7.0 copy-start.6
  19.4 7.1 copy-start.5
  19.4 7.2 copy-start.4
  19.4 9.3 copy-start.7
  389.6 2.0 copy-start
  452.8 35.4 %copy-start.1 = (bf16[1,128,2,128]{3,1,2,0:T(8,128)(2,1)S(1)}, bf16[1,128,2,128]{3,1,2,0:T(8,128)(2,1)}, u32[]{:S(2)}) copy-start(bf16[1,128,2,128]{3,1,2,0:T(8,128)(2,1)} %get-tuple-element.32) | copy-start | bytes 196612
  492.8 3.8 copy-start.2
  492.8 3.8 copy-start.3
where the time goes:
time: 966 us; the launch traced here: 952 us
  local copies, waits for them, and re-layouts  486 us (50%)
  blocking collectives  290 us (30%)
  matrix products  81 us (8%)
  other arithmetic  56.5 us (6%)
  waiting for transfers between devices  36.5 us (4%)
    gather x192, local copies, waits for them, and re-layouts  235 us
    all_to_all x1, blocking collectives, local(): lax.all_to_all(packed, 'tm', split_axis=3, concat_axis=2, tiled=True)  189 us
    all_to_all x1, blocking collectives, local(): lax.all_to_all(lax.all_to_all(packed, 'tm', split_axis=3, concat_axis=2,...  101 us
    unnamed x20, local copies, waits for them, and re-layouts  84.5 us
    dot_general x1, matrix products, correlate(): jnp.einsum('bifck,bjfck->bkij', spectra, partner, preferred_element_type=...  43.3 us
    reshape x2, local copies, waits for them, and re-layouts, local(): received.reshape(band_count, station_count * groups, slices * frames, 2,...  43.2 us
    another operation x5, other arithmetic  40.7 us
    ppermute x1, waiting for transfers between devices, shifted(): lax.ppermute(value, axis, [(source, source + steps) for source in range(f...  36.5 us
  transfers between devices with their start and end apart: 1, of which 1 were waited for; matrix products, arithmetic and copies ran while one was open for 1% of the time, Pallas kernels for 0%

commit v1 on v0

--- a/solution.py
+++ b/solution.py
@@ -11,6 +11,23 @@
 NFRAC = 64
 NPHASE = 1024
 MAXD = 8192
+
+
+def stocks_pass(sample):
+    everything = lax.axis_size("tm")
+    item_now, view_out = (everything, lax.axis_index("tm"))
+    aux = sample.shape[3] // item_now
+    block_now = list(sample.shape)
+    block_now[3] = aux
+    row_out = block_now[2]
+    block_now[2] = row_out * item_now
+    v_now = jnp.zeros(block_now, sample.dtype)
+    for m in range(item_now):
+        carry = lax.dynamic_slice_in_dim(sample, (view_out ^ m) * aux, aux, axis=3)
+        if m:
+            carry = lax.ppermute(carry, "tm", list(map(lambda i: (i, i ^ m), range(item_now))))
+        v_now = lax.dynamic_update_slice_in_dim(v_now, carry, (view_out ^ m) * row_out, axis=2)
+    return v_now
 
 
 def shifted(value, axis, steps):
@@ -153,13 +170,7 @@
     block_width = CHANNELS // (slices * groups)
     spectra = transform(rotated, dft_tables(), block_width)
     packed = spectra.reshape(band_count, station_count, frames, slices, groups, 2 * block_width)
-    received = lax.all_to_all(
-        lax.all_to_all(packed, "tm", split_axis=3, concat_axis=2, tiled=True),
-        "sta",
-        split_axis=4,
-        concat_axis=1,
-        tiled=True,
-    )
+    received = lax.all_to_all(stocks_pass(packed), "sta", split_axis=4, concat_axis=1, tiled=True)
     gathered = received.reshape(band_count, station_count * groups, slices * frames, 2, block_width)
     return correlate(gathered)
 

time: 966 us -> 939 us (0.972)
  the two profiles are of different devices: /device:TPU:0 before, /device:TPU:8 now
where the time goes in v1:
time: 939 us; the launch traced here: 925 us
  local copies, waits for them, and re-layouts  482 us (51%)
  waiting for transfers between devices  195 us (21%)
  blocking collectives  96.9 us (10%)
  matrix products  81 us (9%)
  other arithmetic  56.9 us (6%)
  starting transfers between devices  13.4 us (1%)
    gather x192, local copies, waits for them, and re-layouts  235 us
    ppermute x7, waiting for transfers between devices, stocks_pass(): lax.ppermute(carry, 'tm', list(map(lambda i: (i, i ^ m), range(item_now))))  161 us
    all_to_all x1, blocking collectives, local(): lax.all_to_all(stocks_pass(packed), 'sta', split_axis=4, concat_axis=1, t...  96.9 us
    unnamed x22, local copies, waits for them, and re-layouts  84.6 us
    reshape x2, local copies, waits for them, and re-layouts, local(): received.reshape(band_count, station_count * groups, slices * frames, 2,...  43.3 us
    dot_general x1, matrix products, correlate(): jnp.einsum('bifck,bjfck->bkij', spectra, partner, preferred_element_type=...  43.3 us
    another operation x5, other arithmetic  41.1 us
    ppermute x1, waiting for transfers between devices, shifted(): lax.ppermute(value, axis, [(source, source + steps) for source in range(f...  33.4 us
  transfers between devices with their start and end apart: 8, of which 6 were waited for; matrix products, arithmetic and copies ran while one was open for 3% of the time, Pallas kernels for 0%

profile of v1, /device:TPU:8, one launch (start us, length us, event | category | flops | bytes accessed | tf_op | source)
XLA Modules:
  0.0 925.5 jit_solution(11979893565106930996)
XLA Ops:
  0.0 14.6 %copy.34 = bf16[2,4,16,32768]{3,0,2,1:T(2,128)(2,1)S(1)} copy(bf16[2,4,16,32768]{3,2,1,0:T(8,128)(2,1)} %param.5) | data formatting | bytes 16777216 | tf_op args[0]
  17.6 3.6 collective-permute-start
  21.2 7.0 constant_dynamic-update-slice_fusion
  34.3 33.4 %collective-permute-done = bf16[2,64,8223]{2,0,1:T(2,128)(2,1)S(1)} collective-permute-done((bf16[2,64,8223]{2,0,1:T(2,128)(2,1)}, bf16[2,64,8223]{2,0,1:T(2,128)(2,1)S(1)}, u32[]{:S(2)}, u32[]{:S(2)}) %collective-permute-start) | collective-permute-done | bytes 2105120 | tf_op jit(solution)/shard_map/ppermute | solution.py:36
  67.7 60.9 %dynamic-update-slice.3 = bf16[2,64,41088]{2,0,1:T(2,128)(2,1)} dynamic-update-slice(bf16[2,64,41088]{2,0,1:T(2,128)(2,1)} %constant_dynamic-update-slice_fusion, bf16[2,64,8223]{2,0,1:T(2,128)(2,1)S(1)} %collective-permute-done, s32[]{} %constant.169, s32[]{} %constant.169, s32[]{} %constant.170) | dynamic-update-slice | bytes 4210180
  128.7 10.2 %dynamic-update-slice.4 = bf16[2,64,41088]{2,0,1:T(2,128)(2,1)} dynamic-update-slice(bf16[2,64,41088]{2,0,1:T(2,128)(2,1)} %dynamic-update-slice.3, bf16[2,64,97]{2,0,1:T(2,128)(2,1)S(1)} %broadcast_in_dim.28, s32[]{} %constant.169, s32[]{} %constant.169, s32[]{} %constant.171) | dynamic-update-slice | bytes 49668 | tf_op jit(solution)/shard_map/concatenate | solution.py:164
  138.8 234.7 %while.1 = (s32[]{:T(128)}, bf16[64,2,41088]{2,1,0:T(2,128)(2,1)}, s32[64,3]{0,1:T(4,128)S(1)}, bf16[64,2,32896]{2,1,0:T(2,128)(2,1)}, s32[]{:T(128)}) while((s32[]{:T(128)}, bf16[64,2,41088]{2,1,0:T(2,128)(2,1)}, s32[64,3]{0,1:T(4,128)S(1)}, bf16[64,2,32896]{2,1,0:T(2,128)(2,1)}, s32[]{:T(128)}) %tuple.39), condition=%wide.while_cond, body=%wide.while_body.sunk | while | flops 2 | bytes 264309 | solution.py:54
  373.5 14.2 %reshape.521 = bf16[2,64,257,128]{3,2,0,1:T(8,128)(2,1)} reshape(bf16[2,64,32896]{2,0,1:T(2,128)(2,1)} %bitcast.93) | data formatting | bytes 16842752 | tf_op jit(solution)/shard_map/reshape | solution.py:63
  390.2 11.9 %fusion.6 = f32[64,128,2,256]{3,1,2,0:T(8,128)} fusion(bf16[2,64,257,128]{3,2,0,1:T(8,128)(2,1)} %reshape.521, bf16[64,256,128]{1,2,0:T(8,128)(2,1)S(1)} %bitcast.91), kind=kOutput, calls=%fused_computation.13 | convolution fusion | flops 1073741824 | bytes 27262976 | tf_op jit(solution)/shard_map/crnp,rpv->crnv/dot_general | solution.py:64
  402.1 16.7 %add_bitcast_fusion = f32[2,64,256,128]{2,3,0,1:T(8,128)} fusion(f32[64,128,2,256]{3,1,2,0:T(8,128)} %fusion.6, bf16[2,64,257,128]{3,2,0,1:T(8,128)(2,1)} %reshape.521, bf16[64,256,128]{1,2,0:T(8,128)(2,1)} %bitcast.92), kind=kOutput, calls=%fused_computation.9 | convolution fusion | flops 1077936128 | bytes 44040192 | tf_op jit(solution)/shard_map/crnp,rpv->crnv/dot_general | solution.py:67
  418.8 11.1 %fusion.78 = (f32[1,64,256,128]{2,3,0,1:T(8,128)}, f32[1,64,256,128]{2,3,0,1:T(8,128)}) fusion(f32[2,64,256,128]{2,3,0,1:T(8,128)} %add_bitcast_fusion), kind=kLoop, calls=%fused_computation.146 | loop fusion | bytes 33554432 | tf_op jit(solution)/shard_map/slice | solution.py:82
  429.9 10.9 %squeeze.4 = f32[1,64,2,128,128]{3,2,4,1,0:T(2,128)} reshape(f32[1,64,256,128]{2,3,0,1:T(8,128)} %get-tuple-element.29) | data formatting | bytes 16777216 | tf_op jit(solution)/shard_map/squeeze | solution.py:82
  440.8 10.8 %squeeze.5 = f32[1,64,2,128,128]{3,2,4,1,0:T(2,128)} reshape(f32[1,64,256,128]{2,3,0,1:T(8,128)} %get-tuple-element.30) | data formatting | bytes 16777216 | tf_op jit(solution)/shard_map/squeeze | solution.py:82
  451.5 35.7 %add_convert_fusion.1 = (bf16[1,64,2,128,128]{3,4,0,2,1:T(8,128)(2,1)S(1)}, bf16[1,64,2,128,128]{3,4,0,2,1:T(8,128)(2,1)}) fusion(f32[1,64,2,128,128]{3,2,4,1,0:T(2,128)} %squeeze.5, f32[1,64,2,128,128]{3,2,4,1,0:T(2,128)} %squeeze.4, f32[2,128,128]{1,2,0:T(8,128)S(1)} %convert_multiply_fusion, f32[64]{0:T(128)S(1)} %mul.558, f32[64]{0:T(128)S(1)} %div.46), kind=kLoop, calls=%fused_computation.24 | loop fusion | flops 23068672 | bytes 25297408 | tf_op jit(solution)/shard_map/convert.16
  487.3 4.6 convolution_bitcast_fusion
  491.9 3.8 add_convert_fusion
  495.7 4.6 fusion.14
  500.3 9.8 %copy.43 = bf16[64,2,32,2,4,128]{5,4,3,0,2,1:T(4,128)(2,1)} copy(bf16[64,2,32,2,4,128]{5,2,4,3,1,0:T(8,128)(2,1)S(1)} %fusion.14) | data formatting | bytes 16777216 | tf_op jit(solution)/shard_map/convert_element_type | solution.py:134
  510.1 14.5 %reshape_reshape.3 = bf16[4,16,2,8,4,1024]{5,1,0,4,3,2:T(8,128)(2,1)} reshape(bf16[64,2,32,2,4,128]{5,4,3,0,2,1:T(4,128)(2,1)} %copy.43) | data formatting | bytes 16777216 | tf_op jit(solution)/shard_map/reshape;reshape | solution.py:172
  524.6 6.4 constant_dynamic-slice_fusion.1
  534.8 3.0 collective-permute-start.7
  542.0 58.9 %collective-permute-done.1 = bf16[4,16,2,1,4,1024]{5,1,0,4,3,2:T(8,128)(2,1)} collective-permute-done((bf16[4,16,2,1,4,1024]{5,1,0,4,3,2:T(8,128)(2,1)}, bf16[4,16,2,1,4,1024]{5,1,0,4,3,2:T(8,128)(2,1)}, u32[]{:S(2)}, u32[]{:S(2)}) %collective-permute-start.1) | collective-permute-done | bytes 1048608 | tf_op jit(solution)/shard_map/ppermute | solution.py:28
  608.6 14.3 %collective-permute-done.3 = bf16[4,16,2,1,4,1024]{5,1,0,4,3,2:T(8,128)(2,1)} collective-permute-done((bf16[4,16,2,1,4,1024]{5,1,0,4,3,2:T(8,128)(2,1)}, bf16[4,16,2,1,4,1024]{5,1,0,4,3,2:T(8,128)(2,1)}, u32[]{:S(2)}, u32[]{:S(2)}) %collective-permute-start.3) | collective-permute-done | bytes 1048608 | tf_op jit(solution)/shard_map/ppermute | solution.py:28
  625.9 45.9 %collective-permute-done.4 = bf16[4,16,2,1,4,1024]{5,1,0,4,3,2:T(8,128)(2,1)S(1)} collective-permute-done((bf16[4,16,2,1,4,1024]{5,1,0,4,3,2:T(8,128)(2,1)}, bf16[4,16,2,1,4,1024]{5,1,0,4,3,2:T(8,128)(2,1)S(1)}, u32[]{:S(2)}, u32[]{:S(2)}) %collective-permute-start.4) | collective-permute-done | bytes 1048608 | tf_op jit(solution)/shard_map/ppermute | solution.py:28
  673.7 20.6 %collective-permute-done.5 = bf16[4,16,2,1,4,1024]{5,1,0,4,3,2:T(8,128)(2,1)S(1)} collective-permute-done((bf16[4,16,2,1,4,1024]{5,1,0,4,3,2:T(8,128)(2,1)S(1)}, bf16[4,16,2,1,4,1024]{5,1,0,4,3,2:T(8,128)(2,1)S(1)}, u32[]{:S(2)}, u32[]{:S(2)}) %collective-permute-start.5) | collective-permute-done | bytes 1048608 | tf_op jit(solution)/shard_map/ppermute | solution.py:28
  696.3 21.6 %collective-permute-done.6 = bf16[4,16,2,1,4,1024]{5,1,0,4,3,2:T(8,128)(2,1)S(1)} collective-permute-done((bf16[4,16,2,1,4,1024]{5,1,0,4,3,2:T(8,128)(2,1)S(1)}, bf16[4,16,2,1,4,1024]{5,1,0,4,3,2:T(8,128)(2,1)S(1)}, u32[]{:S(2)}, u32[]{:S(2)}) %collective-permute-start.6) | collective-permute-done | bytes 1048608 | tf_op jit(solution)/shard_map/ppermute | solution.py:28
  721.5 96.9 %all_to_all.15 = bf16[4,16,16,1,4,1024]{5,2,1,0,3,4:T(8,128)(2,1)} all-to-all(bf16[4,16,16,1,4,1024]{5,2,1,0,3,4:T(8,128)(2,1)S(1)} %copy_dynamic-update-slice_fusion), channel_id=1, replica_groups=mesh['tm'=8,'sta'=4] {'sta'}, dimensions={4} | all-to-all | bytes 16777216 | tf_op jit(solution)/shard_map/all_to_all | solution.py:173
  818.4 8.7 copy.52
  827.1 14.5 %reshape.488 = bf16[4,64,16,2,512]{4,3,2,1,0:T(2,128)(2,1)} reshape(bf16[4,4,16,16,1,1,1024]{6,3,2,1,0,5,4:T(8,128)(2,1)} %copy.52) | data formatting | bytes 16777216 | tf_op jit(solution)/shard_map/reshape | solution.py:174
  841.6 28.8 %copy.56 = bf16[4,64,16,2,512]{1,2,3,4,0:T(8,128)(2,1)} copy(bf16[4,64,16,2,512]{4,3,2,1,0:T(2,128)(2,1)} %reshape.488) | data formatting | bytes 16777216 | tf_op jit(solution)/shard_map/reshape | solution.py:174
  870.3 11.6 %slice_negate_fusion = (bf16[4,64,16,1,512]{1,2,3,4,0:T(8,128)(2,1)}, bf16[4,64,16,1,512]{1,2,3,4,0:T(8,128)(2,1)}) fusion(bf16[4,64,16,2,512]{1,2,3,4,0:T(8,128)(2,1)} %copy.56), kind=kLoop, calls=%fused_computation.11 | loop fusion | flops 2097152 | bytes 16777216 | tf_op jit(solution)/shard_map/neg | solution.py:139
  882.0 43.3 %bitcast_multiply_fusion = f32[4,512,64,128]{3,2,1,0:T(8,128)} fusion(bf16[4,64,16,2,512]{1,2,3,4,0:T(8,128)(2,1)} %copy.56, bf16[4,64,16,1,512]{1,2,3,4,0:T(8,128)(2,1)} %get-tuple-element.28, bf16[4,64,16,1,512]{1,2,3,4,0:T(8,128)(2,1)} %get-tuple-element.27), kind=kOutput, calls=%fused_computation.2 | convolution fusion | flops 1140850688 | bytes 83886080 | tf_op jit(solution)/shard_map/bifck,bjfck->bkij/dot_general | solution.py:141
  (250 shorter events, 272.3 us)
Async XLA Ops:
  17.6 50.2 %collective-permute-start = (bf16[2,64,8223]{2,0,1:T(2,128)(2,1)}, bf16[2,64,8223]{2,0,1:T(2,128)(2,1)S(1)}, u32[]{:S(2)}, u32[]{:S(2)}) collective-permute-start(bf16[2,64,8223]{2,0,1:T(2,128)(2,1)} %slice.65), channel_id=1, source_target_pairs={{4,0},{8,4},{12,8},{16,12},{20,16},{24,20},{28,24},{5,1},{9,5},{13... | collective-permute-start | bytes 6315272 | tf_op jit(solution)/shard_map/ppermute | solution.py:36
  21.2 7.0 copy-start.7
  21.2 7.1 copy-start.6
  21.2 7.2 copy-start.5
  21.2 9.4 %copy-start.8 = (s32[16,1]{0,1:T(1,128)S(1)}, s32[16,1]{0,1:T(1,128)}, u32[]{:S(2)}) copy-start(s32[16,1]{0,1:T(1,128)} %param.7) | copy-start | bytes 196
  388.2 2.0 copy-start
  451.5 35.8 %copy-start.2 = (bf16[1,128,2,128]{3,1,2,0:T(8,128)(2,1)S(1)}, bf16[1,128,2,128]{3,1,2,0:T(8,128)(2,1)}, u32[]{:S(2)}) copy-start(bf16[1,128,2,128]{3,1,2,0:T(8,128)(2,1)} %get-tuple-element.40) | copy-start | bytes 196612
  491.8 3.8 copy-start.3
  491.9 3.8 copy-start.4
  531.0 69.9 %collective-permute-start.1 = (bf16[4,16,2,1,4,1024]{5,1,0,4,3,2:T(8,128)(2,1)}, bf16[4,16,2,1,4,1024]{5,1,0,4,3,2:T(8,128)(2,1)}, u32[]{:S(2)}, u32[]{:S(2)}) collective-permute-start(bf16[4,16,2,1,4,1024]{5,1,0,4,3,2:T(8,128)(2,1)} %get-tuple-element.37), channel_id=1, source_target_pairs={{0,4},{4,0},{8,12},{12,8},{16,20},{20,16},{24,28},{28,24},{1,5},{5... | collective-permute-start | bytes 3145736 | tf_op jit(solution)/shard_map/ppermute | solution.py:28
  533.4 70.6 %collective-permute-start.2 = (bf16[4,16,2,1,4,1024]{5,1,0,4,3,2:T(8,128)(2,1)}, bf16[4,16,2,1,4,1024]{5,1,0,4,3,2:T(8,128)(2,1)}, u32[]{:S(2)}, u32[]{:S(2)}) collective-permute-start(bf16[4,16,2,1,4,1024]{5,1,0,4,3,2:T(8,128)(2,1)} %get-tuple-element.36), channel_id=1, source_target_pairs={{0,8},{4,12},{8,0},{12,4},{16,24},{20,28},{24,16},{28,20},{1,9},{5... | collective-permute-start | bytes 3145736 | tf_op jit(solution)/shard_map/ppermute | solution.py:28
  533.8 89.1 %collective-permute-start.3 = (bf16[4,16,2,1,4,1024]{5,1,0,4,3,2:T(8,128)(2,1)}, bf16[4,16,2,1,4,1024]{5,1,0,4,3,2:T(8,128)(2,1)}, u32[]{:S(2)}, u32[]{:S(2)}) collective-permute-start(bf16[4,16,2,1,4,1024]{5,1,0,4,3,2:T(8,128)(2,1)} %get-tuple-element.35), channel_id=1, source_target_pairs={{0,12},{4,8},{8,4},{12,0},{16,28},{20,24},{24,20},{28,16},{1,13},{... | collective-permute-start | bytes 3145736 | tf_op jit(solution)/shard_map/ppermute | solution.py:28
  534.8 66.1 %copy-start.1 = (bf16[4,16,2,1,4,1024]{5,1,0,4,3,2:T(8,128)(2,1)S(1)}, bf16[4,16,2,1,4,1024]{5,1,0,4,3,2:T(8,128)(2,1)}, u32[]{:S(2)}) copy-start(bf16[4,16,2,1,4,1024]{5,1,0,4,3,2:T(8,128)(2,1)} %get-tuple-element.33) | copy-start | bytes 3145732
  534.8 184.8 %collective-permute-start.7 = (bf16[4,16,2,1,4,1024]{5,1,0,4,3,2:T(8,128)(2,1)S(1)}, bf16[4,16,2,1,4,1024]{5,1,0,4,3,2:T(8,128)(2,1)S(1)}, u32[]{:S(2)}, u32[]{:S(2)}) collective-permute-start(bf16[4,16,2,1,4,1024]{5,1,0,4,3,2:T(8,128)(2,1)S(1)} %get-tuple-element.31), channel_id=1, source_target_pairs={{0,28},{4,24},{8,20},{12,16},{16,12},{20,8},{24,4},{28,0},{1,29},{... | collective-permute-start | bytes 3145736 | tf_op jit(solution)/shard_map/ppermute | solution.py:28
  537.9 134.0 %collective-permute-start.4 = (bf16[4,16,2,1,4,1024]{5,1,0,4,3,2:T(8,128)(2,1)}, bf16[4,16,2,1,4,1024]{5,1,0,4,3,2:T(8,128)(2,1)S(1)}, u32[]{:S(2)}, u32[]{:S(2)}) collective-permute-start(bf16[4,16,2,1,4,1024]{5,1,0,4,3,2:T(8,128)(2,1)} %get-tuple-element.34), channel_id=1, source_target_pairs={{0,16},{4,20},{8,24},{12,28},{16,0},{20,4},{24,8},{28,12},{1,17},{... | collective-permute-start | bytes 3145736 | tf_op jit(solution)/shard_map/ppermute | solution.py:28
  600.9 93.3 %collective-permute-start.5 = (bf16[4,16,2,1,4,1024]{5,1,0,4,3,2:T(8,128)(2,1)S(1)}, bf16[4,16,2,1,4,1024]{5,1,0,4,3,2:T(8,128)(2,1)S(1)}, u32[]{:S(2)}, u32[]{:S(2)}) collective-permute-start(bf16[4,16,2,1,4,1024]{5,1,0,4,3,2:T(8,128)(2,1)S(1)} %copy-done.1), channel_id=1, source_target_pairs={{0,20},{4,16},{8,28},{12,24},{16,4},{20,0},{24,12},{28,8},{1,21},{... | collective-permute-start | bytes 3145736 | tf_op jit(solution)/shard_map/ppermute | solution.py:28
  604.0 113.9 %collective-permute-start.6 = (bf16[4,16,2,1,4,1024]{5,1,0,4,3,2:T(8,128)(2,1)S(1)}, bf16[4,16,2,1,4,1024]{5,1,0,4,3,2:T(8,128)(2,1)S(1)}, u32[]{:S(2)}, u32[]{:S(2)}) collective-permute-start(bf16[4,16,2,1,4,1024]{5,1,0,4,3,2:T(8,128)(2,1)S(1)} %get-tuple-element.32), channel_id=1, source_target_pairs={{0,24},{4,28},{8,16},{12,20},{16,8},{20,12},{24,0},{28,4},{1,25},{... | collective-permute-start | bytes 3145736 | tf_op jit(solution)/shard_map/ppermute | solution.py:28
